TPU v7x, 512 devices: a whole 4x8x8 slice. The times are simulated.
512 devices in a mesh: section: 8 (over y_lo, core), dp: 64 (over y_hi, x, z).
Axes of the slice: x: 4, y: 8 (y_hi: 2, y_lo: 4; y = y_hi * 4 + y_lo), z: 8, core: 2. Of those that a mesh axis runs over, the one named last changes fastest.
Arguments:
- acts: bfloat16 [8, 64, 1, 64, 2, 2, 128], P('section', 'dp'), may hold values from -6 to 6
- preacts: bfloat16 [8, 64, 1, 64, 2, 2, 128], P('section', 'dp'), may hold values from -6 to 6
- top_grad: bfloat16 [64, 1, 64, 2, 2, 128], P('dp'), may hold values from -6 to 6
- weights: bfloat16 [8, 64, 1728], P('section'), may hold values from -0.21875 to 0.21875
- a_factor: bfloat16 [8, 1728, 1728], P('section', 'dp'), as said below
- g_factor: bfloat16 [8, 64, 64], P('section'), as said below
Outputs:
- act_grads: bfloat16 [8, 64, 1, 64, 2, 2, 128], P('section', 'dp')
- update: float32 [8, 1728, 64], P('section', 'dp')
- inverse: float32 [8, 1728, 1728], P('section', 'dp')
Inputs may be any that keep to these rules, and one draw needn't show every extreme that they name: `a_factor`: each matrix is symmetric and positive definite. `g_factor`: each matrix is symmetric and positive definite.
All inputs are finite; a program needn't handle non-finite values. Where the computation divides by a largest or mean magnitude, that divisor is 1e-20 or more.
Results may differ from a plain program's by a relative error of at most 0.006.
Values may be sent and summed in bfloat16 or wider, within the bound.
A program may use at most 64 MiB of HBM per device.

v0:
```python
import jax
import jax.numpy as jnp
from jax import lax
from jax.sharding import PartitionSpec as P

KW = 3
MICRO = 1


def shifted(value, axis, steps):
    count = lax.axis_size(axis)
    first, last = (max(0, -steps), min(count, count - steps))
    return lax.ppermute(value, axis, [(source, source + steps) for source in range(first, last)])


def tap_offsets(kernel_width):
    middle = kernel_width // 2
    result = []
    for along_x in range(kernel_width):
        for along_y in range(kernel_width):
            for along_z in range(kernel_width):
                result.append((along_x - middle, along_y - middle, along_z - middle))
    return result


def taps_stack(volume, kernel_width, direction):
    middle = kernel_width // 2
    padded = jnp.pad(volume, ((0, 0), (middle, middle), (middle, middle), (middle, middle)))
    size_x, size_y, size_z = (volume.shape[1], volume.shape[2], volume.shape[3])
    pieces = []
    for off_x, off_y, off_z in tap_offsets(kernel_width):
        start_x = middle + direction * off_x
        start_y = middle + direction * off_y
        start_z = middle + direction * off_z
        pieces.append(
            padded[
                :,
                start_x : start_x + size_x,
                start_y : start_y + size_y,
                start_z : start_z + size_z,
            ]
        )
    stacked = jnp.stack(pieces, 0)
    return stacked.reshape(len(pieces) * volume.shape[0], size_x * size_y * size_z)


def back_input(grad_out, w_rows):
    columns = taps_stack(grad_out, KW, -1)
    summed = lax.dot_general(
        w_rows, columns, (((0,), (0,)), ((), ())), preferred_element_type=jnp.float32
    )
    return summed.astype(jnp.bfloat16).reshape(grad_out.shape)


def back_weight(volume, grad_out):
    columns = taps_stack(volume, KW, 1)
    flattened = grad_out.reshape(grad_out.shape[0], -1)
    return lax.dot_general(
        columns, flattened, (((1,), (1,)), ((), ())), preferred_element_type=jnp.float32
    )


def local_inverse(matrix):
    values = matrix.astype(jnp.float32)
    step_size = 1.0 / jnp.max(jnp.sum(jnp.abs(values), axis=1))
    identity = jnp.eye(matrix.shape[0], dtype=jnp.float32)
    resid0 = (identity - step_size * values).astype(jnp.bfloat16)
    resid1 = jnp.dot(resid0, resid0, preferred_element_type=jnp.float32).astype(jnp.bfloat16)
    cross_term = jnp.dot(resid1, resid0, preferred_element_type=jnp.float32)
    return step_size * (
        identity + resid0.astype(jnp.float32) + resid1.astype(jnp.float32) + cross_term
    )


def eye_rows(start_row, row_total, order_full):
    column_ids = lax.broadcasted_iota(jnp.int32, (row_total, order_full), 1)
    row_ids = lax.broadcasted_iota(jnp.int32, (row_total, order_full), 0)
    return (column_ids == start_row + row_ids).astype(jnp.float32)


def shards(acts, preacts, top_grad, weights, a_factor, g_factor):
    section_index = lax.axis_index("section")
    section_count = lax.axis_size("section")
    tick_count = MICRO + section_count - 1
    inputs = acts[0, 0]
    pre_values = preacts[0, 0]
    upper_grads = top_grad[0]
    channels = weights.shape[1]
    w_rows = weights[0].reshape(channels, -1, channels).transpose(1, 0, 2).reshape(-1, channels)
    zero_field = jnp.zeros(inputs.shape[1:], jnp.bfloat16)

    def one_tick(tick_index, carried):
        outgoing, stored_grads, stored_slopes = carried
        incoming = shifted(outgoing, "section", -1)
        micro_index = tick_index - (section_count - 1 - section_index)
        is_valid = jnp.logical_and(micro_index >= 0, micro_index < MICRO)
        clipped = jnp.clip(micro_index, 0, MICRO - 1)
        from_top = lax.dynamic_index_in_dim(upper_grads, clipped, 0, keepdims=False)
        arriving = jnp.where(section_index == section_count - 1, from_top, incoming)
        pre_now = lax.dynamic_index_in_dim(pre_values, clipped, 0, keepdims=False)
        grad_out = jnp.where(pre_now > 0, arriving, zero_field)
        sending = back_input(grad_out, w_rows)
        old_grad = lax.dynamic_index_in_dim(stored_grads, clipped, 0, keepdims=False)
        old_slope = lax.dynamic_index_in_dim(stored_slopes, clipped, 0, keepdims=False)
        stored_grads = lax.dynamic_update_index_in_dim(
            stored_grads, jnp.where(is_valid, sending, old_grad), clipped, 0
        )
        stored_slopes = lax.dynamic_update_index_in_dim(
            stored_slopes, jnp.where(is_valid, grad_out, old_slope), clipped, 0
        )
        return (sending, stored_grads, stored_slopes)

    start_state = (
        zero_field,
        jnp.zeros(inputs.shape, jnp.bfloat16),
        jnp.zeros(inputs.shape, jnp.bfloat16),
    )
    last_sent, stored_grads, stored_slopes = lax.fori_loop(0, tick_count, one_tick, start_state)
    local_grad = back_weight(inputs[0], stored_slopes[0])
    summed_grad = lax.psum(local_grad, "dp")
    mean_grad = summed_grad / lax.axis_size("dp")
    a_rows = a_factor[0]
    row_total = a_rows.shape[0]
    order_full = a_rows.shape[1]
    first_row = lax.axis_index("dp") * row_total
    local_max = jnp.max(jnp.sum(jnp.abs(a_rows.astype(jnp.float32)), axis=1))
    step_size = 1.0 / lax.pmax(local_max, "dp")
    own_eye = eye_rows(first_row, row_total, order_full)
    resid0 = (own_eye - step_size * a_rows.astype(jnp.float32)).astype(jnp.bfloat16)
    left_cols = resid0
    resid1 = jnp.dot(
        left_cols,
        lax.all_gather(resid0, "dp", axis=0, tiled=True),
        preferred_element_type=jnp.float32,
    ).astype(jnp.bfloat16)
    left_cols = resid1
    cross_term = jnp.dot(
        left_cols,
        lax.all_gather(resid0, "dp", axis=0, tiled=True),
        preferred_element_type=jnp.float32,
    )
    inverse_rows = step_size * (
        own_eye + resid0.astype(jnp.float32) + resid1.astype(jnp.float32) + cross_term
    )
    g_inverse = local_inverse(g_factor[0])
    preconditioned = jnp.dot(
        mean_grad, g_inverse, precision=lax.Precision.HIGHEST, preferred_element_type=jnp.float32
    )
    update_rows = jnp.dot(
        inverse_rows,
        preconditioned,
        precision=lax.Precision.HIGHEST,
        preferred_element_type=jnp.float32,
    )
    return (stored_grads[None, None], update_rows[None], inverse_rows[None])


def solution(mesh):
    placed = (
        P("section", "dp", None, None, None, None, None),
        P("section", "dp", None, None, None, None, None),
        P("dp", None, None, None, None, None),
        P("section", None, None),
        P("section", "dp", None),
        P("section", None, None),
    )
    return jax.shard_map(
        shards,
        mesh=mesh,
        in_specs=placed,
        out_specs=(
            P("section", "dp", None, None, None, None, None),
            P("section", "dp", None),
            P("section", "dp", None),
        ),
        check_vma=False,
    )
```

profile of v0, /device:TPU:6, one launch (start us, length us, event | category | flops | bytes accessed | tf_op | source)
XLA Modules:
  0.0 1167.6 jit_solution(344950697189547581)
XLA Ops:
  13.1 2.1 reshape.70
  16.6 112.9 %while.20 = (s32[]{:T(128)}, bf16[64,2,2,128]{3,2,1,0:T(2,128)(2,1)}, bf16[1,64,2,2,128]{4,3,2,1,0:T(2,128)(2,1)}, bf16[1,64,2,2,128]{4,3,2,1,0:T(2,128)(2,1)}, ...) while((s32[]{:T(128)}, ...), condition=%wide.region_1.2_spmd.clone, body=%wide.region_0.1_spmd.clone.sunk | while | flops 113475592 | bytes 10772739 | solution.py:118
  17.9 2.0 collective-permute-done
  19.9 1.7 fusion.173
  29.9 3.9 collective-permute-done
  33.9 1.7 fusion.173
  39.7 1.5 fusion.200
  43.9 4.5 collective-permute-done
  48.4 1.7 fusion.173
  54.1 1.5 fusion.200
  58.4 4.5 collective-permute-done
  62.8 1.7 fusion.173
  68.6 1.5 fusion.200
  72.8 4.5 collective-permute-done
  77.3 1.7 fusion.173
  83.1 1.5 fusion.200
  87.3 4.5 collective-permute-done
  91.8 1.7 fusion.173
  97.6 1.5 fusion.200
  101.8 4.5 collective-permute-done
  106.3 1.7 fusion.173
  112.1 1.5 fusion.200
  116.3 4.5 collective-permute-done
  120.8 1.7 fusion.173
  126.6 1.5 fusion.200
  131.0 2.9 fusion.129
  134.0 194.4 %pmax.7 = f32[]{:T(128)} all-reduce(f32[]{:T(128)} %reduce_max.18), channel_id=1, replica_groups=mesh['section'=8,'dp'=64] {'dp'}, use_global_device_ids=true, to_apply=%region_4.5 | all-reduce | flops 1 | bytes 8 | tf_op jit(solution)/shard_map/pmax | solution.py:127
  331.5 613.0 %all-reduce.4.cloned.1.call-done = f32[1728,64]{0,1:T(8,128)} async-done(((f32[1728,64]{0,1:T(8,128)}), f32[1728,64]{0,1:T(8,128)}) %all-reduce.4.cloned.1.call-update) | async-done | bytes 442384 | tf_op jit(solution)/shard_map/psum | solution.py:120
  944.4 1.6 fusion.56
  946.0 197.8 %all-gather.3.cloned.1.call-done = bf16[64,27,1728]{2,1,0:T(8,128)(2,1)} async-done(((bf16[1,27,1728]{2,1,0:T(8,128)(2,1)}), bf16[64,27,1728]{2,1,0:T(8,128)(2,1)}) %all-gather.3.cloned.1.call-update) | async-done | bytes 5971984 | tf_op jit(solution)/shard_map/all_gather | solution.py:133
  1143.8 9.3 reshape.72
  1153.1 4.0 convolution_convert_fusion.1
  (348 shorter events, 69.7 us)
Async XLA Ops:
  7.2 2.5 copy-start.2
  7.2 2.6 copy-start.1
  7.2 937.2 %all-reduce.4.cloned.1.call-start = ((), (), s32[]{:S(2)}) async-start(), calls=%async_computation | async-start | bytes 917504 | tf_op jit(solution)/shard_map/psum | solution.py:120
  16.6 3.3 collective-permute-start
  25.7 2.2 copy-start.4
  28.0 0.6 copy-start.5
  28.6 5.2 collective-permute-start
  39.6 2.2 copy-start.4
  41.9 0.6 copy-start.5
  42.6 5.8 collective-permute-start
  54.1 2.2 copy-start.4
  56.4 0.6 copy-start.5
  57.1 5.8 collective-permute-start
  68.6 2.2 copy-start.4
  70.9 0.6 copy-start.5
  71.5 5.8 collective-permute-start
  83.1 2.2 copy-start.4
  85.4 0.6 copy-start.5
  86.0 5.8 collective-permute-start
  97.6 2.2 copy-start.4
  99.9 0.6 copy-start.5
  100.5 5.8 collective-permute-start
  112.1 2.2 copy-start.4
  114.4 0.6 copy-start.5
  115.0 5.8 collective-permute-start
  126.5 2.2 copy-start.4
  128.8 0.6 copy-start.5
  129.5 199.5 %copy-start.3 = (bf16[1,27,1728]{2,1,0:T(8,128)(2,1)S(1)}, bf16[1,27,1728]{2,1,0:T(8,128)(2,1)}, u32[]{:S(2)}) copy-start(bf16[1,27,1728]{2,1,0:T(8,128)(2,1)} %param.12) | copy-start | bytes 279940
  129.5 200.3 %copy-start.6 = (bf16[1,64,64]{2,1,0:T(8,128)(2,1)S(1)}, bf16[1,64,64]{2,1,0:T(8,128)(2,1)}, u32[]{:S(2)}) copy-start(bf16[1,64,64]{2,1,0:T(8,128)(2,1)} %param.13) | copy-start | bytes 24580
  133.9 1009.9 %all-gather.3.cloned.1.call-start = ((), (), s32[]{:S(2)}) async-start(), calls=%async_computation.1 | async-start | bytes 7454720 | tf_op jit(solution)/shard_map/all_gather | solution.py:133
  1153.1 4.5 copy-start
Sparse Core Ops, SparseCore 0:
  134.0 810.3 all-reduce.3
  950.3 193.4 all-gather.2
where the time goes:
time: 1170 us
  waiting for transfers between devices  844 us (72%)
  blocking collectives  194 us (17%)
  local copies, waits for them, and re-layouts  64.3 us (5%)
  matrix products  22.2 us (2%)
  other arithmetic  16.6 us (1%)
  between operations  15.5 us (1%)
    psum x1, waiting for transfers between devices, shards(): summed_grad = lax.psum(local_grad, 'dp')  613 us
    all_gather x1, waiting for transfers between devices, shards(): lax.all_gather(resid0, 'dp', axis=0, tiled=True)  198 us
    pmax x1, blocking collectives, shards(): step_size = 1.0 / lax.pmax(local_max, 'dp')  194 us
    ppermute x8, waiting for transfers between devices, shifted(): lax.ppermute(value, axis, [(source, source + steps) for source in range(f...  32.9 us
    while x240, local copies, waits for them, and re-layouts  30.6 us
  transfers between devices with their start and end apart: 10, of which 10 were waited for; matrix products, arithmetic and copies ran while one was open for 0% of the time, Pallas kernels for 0%

commit v1 on v0

v1 whole, which is shorter than its diff:
```python
import functools

import jax
import jax.numpy as jnp
from jax import lax
from jax.experimental import pallas as pl
from jax.experimental.pallas import tpu as pltpu
from jax.sharding import PartitionSpec as P

MESH = pl.DeviceIdType.MESH
F32 = jnp.float32
BF16 = jnp.bfloat16
HIGH = lax.Precision.HIGHEST

ORDER = 1728
PAIRED = [((a, 2, c), (a, 0, c)) for a in range(3) for c in range(3)]
MIDDLE = [(a, 1, c) for a in range(3) for c in range(3)]
PAIRED += [(MIDDLE[2 * m], MIDDLE[min(2 * m + 1, 8)]) for m in range(5)]
TILES = len(PAIRED)


def tap_of(abc):
    return (abc[0] * 3 + abc[1]) * 3 + abc[2]


def iota(shape, dim):
    return lax.broadcasted_iota(jnp.int32, shape, dim)


def ones_where(mask):
    return jnp.where(mask, 1.0, 0.0).astype(BF16)


def mm(left, right, precision=None):
    return lax.dot_general(
        left, right, (((1,), (0,)), ((), ())), precision=precision, preferred_element_type=F32
    )


def mm_nt(left, right):
    return lax.dot_general(left, right, (((1,), (1,)), ((), ())), preferred_element_type=F32)


def pad_to(value, step):
    return -(-value // step) * step


def kernel(cfg, acts, pre, top, w, a, gf, og, ou, oi, *scratch):
    (
        wt, bw, pre_p, top_p, ash, arr, obuf, gcat, own, apad, sel, piece, spc, mx,
        rcol32, rcol, pbuf, prc, xf, xcat, wg, rg, sbuf, rs, pch, pag, pall,
        gbd,
        ch_s, ch_r, fa_s, fa_r, sa_s, sa_r, sm_s, sm_r, pr_s, pr_r,
        gr_s, gr_r, rr_s, rr_r, as_s, as_r, af_s, af_r,
    ) = scratch
    n_sec, nf, ns, rows, rpad, early = cfg
    blk = rows * nf
    cw = sel.shape[1]
    frows = rg.shape[1]
    srows = rs.shape[1]
    sec = lax.axis_index("section")
    dp = lax.axis_index("dp")
    fi = lax.rem(dp, nf)
    si = dp // nf

    def f_peer(k):
        return lax.rem(fi + k, nf)

    def f_from(k):
        return lax.rem(fi - k + nf, nf)

    def s_peer(k):
        return lax.rem(si + k, ns)

    def s_from(k):
        return lax.rem(si - k + ns, ns)

    def f_dev(index):
        return (sec, si * nf + index)

    def s_dev(index):
        return (sec, index * nf + fi)

    def copy_to(src, dst, ss, rr, k, device):
        return pltpu.make_async_remote_copy(
            src_ref=src, dst_ref=dst, send_sem=ss.at[k - 1], recv_sem=rr.at[k - 1],
            device_id=device, device_id_type=MESH,
        )

    def each(count, body):
        lax.fori_loop(1, count, lambda k, carry: (body(k), carry)[1], 0)

    barrier = pltpu.get_barrier_semaphore()
    each(nf, lambda k: pl.semaphore_signal(barrier, inc=1, device_id=f_dev(f_peer(k)), device_id_type=MESH))
    each(ns, lambda k: pl.semaphore_signal(barrier, inc=1, device_id=s_dev(s_peer(k)), device_id_type=MESH))

    for near in (sec + 1, sec + n_sec - 1):
        pl.semaphore_signal(
            barrier, inc=1, device_id=(lax.rem(near, n_sec), dp), device_id_type=MESH
        )

    own[...] = jnp.zeros_like(own)
    own[0:rows, :] = a[...]
    pl.semaphore_wait(barrier, nf + ns)

    def fa_copy(k, slot, index):
        return copy_to(own, apad.at[slot], fa_s, fa_r, k, f_dev(index))

    each(nf, lambda k: fa_copy(k, fi, f_peer(k)).start())
    apad[fi] = own[...]

    wpair = jnp.concatenate([w[...], w[...]], axis=0).astype(F32)
    for m in range(ORDER // 128):
        wt[128 * m : 128 * m + 128, :] = wpair[:, 128 * m : 128 * m + 128].T
    last = 128 * (ORDER // 128)
    wt[last:ORDER, :] = wpair[:, last:ORDER].T
    left64 = iota((64, 128), 1) < 64

    def wtap(aa, b, c):
        start = 64 * tap_of((aa, b, c))
        return wt[start : start + 64, :]

    for c in range(3):
        for x in range(2):
            for y in range(2):
                for x2 in range(2):
                    block = jnp.where(left64, wtap(x - x2 + 1, y + 1, c), wtap(x - x2 + 1, y, c))
                    row = 64 * (2 * x + y)
                    lane = 256 * c + 128 * x2
                    bw[row : row + 64, lane : lane + 128] = block.astype(BF16)

    out_row, in_row = (iota((256, 256), 0), iota((256, 256), 1))
    perm = ones_where(in_row == (out_row & 63) * 4 + (out_row >> 6))
    pre_p[...] = mm(perm, pre[...])
    top_p[...] = mm(perm, top[...])
    lanes = iota((256, 128), 1)
    act_p = mm(perm, acts[...])
    ash[0:256, :] = jnp.where(lanes == 0, 0.0, pltpu.roll(act_p, 1, 1)).astype(BF16)
    ash[256:512, :] = act_p.astype(BF16)
    ash[512:768, :] = jnp.where(lanes == 127, 0.0, pltpu.roll(act_p, 127, 1)).astype(BF16)

    def send_chain():
        return pltpu.make_async_remote_copy(
            src_ref=obuf, dst_ref=arr, send_sem=ch_s, recv_sem=ch_r,
            device_id=(lax.rem(sec - 1 + n_sec, n_sec), dp), device_id_type=MESH,
        )

    def gr_copy(k, chunk, slot):
        return copy_to(
            wg.at[pl.ds(pl.multiple_of(chunk * frows, frows), frows), :], rg.at[slot],
            gr_s, gr_r, k, f_dev(chunk),
        )

    def holds(chunk):
        return chunk * frows < TILES * 64

    def relay():
        @pl.when(sec < n_sec - 1)
        def _():
            send_chain().wait_recv()
            top_p[...] = arr[...].astype(F32)

        lane = iota((256, 128), 1)
        grad = jnp.where(pre_p[...] > 0, top_p[...], 0.0)
        gcat[256:512, :] = grad.astype(BF16)
        gcat[0:256, :] = jnp.where(lane == 127, 0.0, pltpu.roll(grad, 127, 1)).astype(BF16)
        gcat[512:768, :] = jnp.where(lane == 0, 0.0, pltpu.roll(grad, 1, 1)).astype(BF16)
        obuf[...] = mm(bw[...], gcat[...]).astype(BF16)

        @pl.when(sec > 0)
        def _():
            send_chain().start()

        back_row, back_col = (iota((256, 256), 0), iota((256, 256), 1))
        back = ones_where(back_row == (back_col & 63) * 4 + (back_col >> 6))
        og[...] = mm(back, obuf[...]).astype(BF16)

        full = mm_nt(ash[...], gcat[256:512, :])
        left = iota((64, 128), 1) < 64

        def part(aa, c, y):
            total = None
            for x in range(2):
                x2 = x - (aa - 1)
                if 0 <= x2 < 2:
                    row = 256 * c + 64 * (2 * x + y)
                    term = full[row : row + 64, 128 * x2 : 128 * x2 + 128]
                    total = term if total is None else total + term
            return total

        parts = {(aa, c, y): part(aa, c, y) for aa in range(3) for c in range(3) for y in range(2)}
        for m, (one, two) in enumerate(PAIRED):
            if one[1] == 2:
                tile = jnp.where(left, parts[one[0], one[2], 1], parts[one[0], one[2], 0])
            else:
                first = parts[one[0], one[2], 0] + pltpu.roll(parts[one[0], one[2], 1], 64, 1)
                second = pltpu.roll(parts[two[0], two[2], 0], 64, 1) + parts[two[0], two[2], 1]
                tile = jnp.where(left, first, second)
            wg[64 * m : 64 * m + 64, :] = tile.astype(wg.dtype)

        def start(k):
            @pl.when(holds(f_peer(k)))
            def _():
                gr_copy(k, f_peer(k), fi).start()

        each(nf, start)

    if wg.shape[0] > 64 * TILES:
        wg[64 * TILES :, :] = jnp.zeros((wg.shape[0] - 64 * TILES, 128), wg.dtype)

    @pl.when(sec >= early)
    def _():
        relay()

    dup = ones_where(iota((64, 128), 0) == (iota((64, 128), 1) & 63))
    dup_t = ones_where(iota((128, 64), 1) == (iota((128, 64), 0) & 63))
    wide = mm(mm(dup_t, gf[...]).astype(BF16), dup)
    g_row, g_col = (iota((128, 128), 0), iota((128, 128), 1))
    values = jnp.where((g_row >> 6) == (g_col >> 6), wide, 0.0)
    g_step = 1.0 / jnp.max(jnp.sum(jnp.abs(values), axis=1, keepdims=True), axis=0, keepdims=True)
    g_eye = jnp.where(g_row == g_col, 1.0, 0.0)
    g_res0 = (g_eye - g_step * values).astype(BF16)
    g_res1 = mm(g_res0, g_res0).astype(BF16)
    gbd[...] = g_step * (g_eye + g_res0.astype(F32) + g_res1.astype(F32) + mm(g_res1, g_res0))

    sel[...] = ones_where((iota((ORDER, cw), 0) == fi * blk + iota((ORDER, cw), 1)) & (iota((ORDER, cw), 1) < blk))

    each(nf, lambda k: fa_copy(k, f_from(k), f_peer(k)).wait_recv())
    rows_all = apad[...].reshape(nf * rpad, ORDER)
    row_sums = jnp.sum(jnp.abs(rows_all.astype(F32)), axis=1, keepdims=True)
    piece[...] = mm(rows_all, sel[...]).astype(BF16)
    mx[si] = jnp.broadcast_to(jnp.max(row_sums, axis=0, keepdims=True), (8, 128))

    def sa_copy(k, slot, index):
        return copy_to(piece, spc.at[slot], sa_s, sa_r, k, s_dev(index))

    def sm_copy(k, slot, index):
        return copy_to(mx.at[si], mx.at[slot], sm_s, sm_r, k, s_dev(index))

    each(ns, lambda k: sm_copy(k, si, s_peer(k)).start())
    each(ns, lambda k: sa_copy(k, si, s_peer(k)).start())
    spc[si] = piece[...]
    each(ns, lambda k: sm_copy(k, s_from(k), s_peer(k)).wait_recv())
    each(ns, lambda k: sa_copy(k, s_from(k), s_peer(k)).wait_recv())
    largest = jnp.max(jnp.max(mx[...], axis=0), axis=0, keepdims=True)[:, 0:1]
    step = 1.0 / largest

    squeeze_row, squeeze_col = (iota((blk, nf * rpad), 0), iota((blk, nf * rpad), 1))
    in_slot = lax.rem(squeeze_col, rpad)
    squeeze = ones_where(((squeeze_col // rpad) * rows + in_slot == squeeze_row) & (in_slot < rows))
    for h in range(ns):
        rcol32[h * blk : h * blk + blk, :] = mm(squeeze, spc[h])
    col_row, col_col = (iota((ORDER, cw), 0), iota((ORDER, cw), 1))
    col_eye = jnp.where((col_row == fi * blk + col_col) & (col_col < blk), 1.0, 0.0)
    rcol[...] = (col_eye - step * rcol32[...]).astype(BF16)

    local = iota((nf * rpad, ORDER), 0)
    slot_row = lax.rem(local, rpad)
    row_eye = jnp.where(
        (iota((nf * rpad, ORDER), 1) == si * blk + (local // rpad) * rows + slot_row) & (slot_row < rows), 1.0, 0.0
    )
    rrow = (row_eye - step * apad[...].reshape(nf * rpad, ORDER).astype(F32)).astype(BF16)
    square = mm(rrow, rcol[...]).astype(BF16)
    partial = mm_nt(square, rcol[...]) + mm_nt(square, sel[...])
    pbuf[...] = partial.astype(BF16).reshape(pbuf.shape)

    def pr_copy(k, chunk, slot):
        return copy_to(pbuf.at[chunk], prc.at[slot], pr_s, pr_r, k, f_dev(chunk))

    each(nf, lambda k: pr_copy(k, f_peer(k), fi).start())
    prc[fi] = pbuf[fi]
    each(nf, lambda k: pr_copy(k, f_peer(k), f_from(k)).wait_recv())

    own_row = iota((rpad, ORDER), 0)
    own_eye = jnp.where((iota((rpad, ORDER), 1) == dp * rows + own_row) & (own_row < rows), 1.0, 0.0)
    own_res = (own_eye - step * own[...].astype(F32)).astype(BF16).astype(F32)
    summed = prc[0].astype(F32)
    for k in range(1, nf):
        summed = summed + prc[k].astype(F32)
    inverse = step * (own_eye + own_res + summed)
    oi[:, 0, :] = inverse[0:rows, :]

    xf[...] = jnp.zeros_like(xf)
    xf[:, 0:ORDER] = inverse
    left_x = iota((rpad, 128), 1) < 64

    def tap_lanes(abc, half):
        tap = tap_of(abc)
        group = xf[:, 128 * (tap // 2) : 128 * (tap // 2) + 128]
        return group if tap % 2 == half else pltpu.roll(group, 64, 1)

    for side in range(2):
        for m in range(TILES // 2):
            one, two = (PAIRED[2 * m][side], PAIRED[2 * m + 1][side])
            tile = jnp.where(left_x, tap_lanes(one, 0), tap_lanes(two, 1))
            if side == 1 and 2 * m + 1 == TILES - 1:
                tile = jnp.where(left_x, tile, 0.0)
            high = tile.astype(BF16)
            low = (tile - high.astype(F32)).astype(BF16)
            xcat[2 * side * rpad : 2 * side * rpad + rpad, 128 * m : 128 * m + 128] = high
            xcat[2 * side * rpad + rpad : 2 * side * rpad + 2 * rpad, 128 * m : 128 * m + 128] = low

    @pl.when(sec < early)
    def _():
        relay()

    @pl.when(holds(fi))
    def _():
        rg[fi] = wg[pl.ds(pl.multiple_of(fi * frows, frows), frows), :]
        each(nf, lambda k: gr_copy(k, fi, f_from(k)).wait_recv())
        total = rg[0].astype(F32)
        for k in range(1, nf):
            total = total + rg[k].astype(F32)
        sbuf[...] = total.reshape(sbuf.shape)

        def rr_copy(k, chunk, slot):
            return copy_to(sbuf.at[chunk], rs.at[slot], rr_s, rr_r, k, s_dev(chunk))

        each(ns, lambda k: rr_copy(k, s_peer(k), si).start())
        rs[si] = sbuf[si]
        each(ns, lambda k: rr_copy(k, s_peer(k), s_from(k)).wait_recv())
        grad_sum = rs[0]
        for k in range(1, ns):
            grad_sum = grad_sum + rs[k]
        mean = grad_sum / (nf * ns)
        pch[...] = mm(mean, gbd[...], HIGH).astype(BF16)

        def as_copy(k, slot, index):
            return copy_to(pch, pag.at[slot], as_s, as_r, k, s_dev(index))

        each(ns, lambda k: as_copy(k, si, s_peer(k)).start())
        pag[si] = pch[...]
        each(ns, lambda k: as_copy(k, s_from(k), s_peer(k)).wait_recv())
        pall[fi] = pag[...].reshape(frows, 128)
        each(ns, lambda k: rr_copy(k, s_peer(k), si).wait_send())
        each(ns, lambda k: as_copy(k, si, s_peer(k)).wait_send())

    def af_copy(k, slot, index):
        return copy_to(pall.at[fi], pall.at[slot], af_s, af_r, k, f_dev(index))

    @pl.when(holds(fi))
    def _():
        each(nf, lambda k: af_copy(k, fi, f_peer(k)).start())

    def af_wait(k):
        @pl.when(holds(f_from(k)))
        def _():
            af_copy(k, f_from(k), f_peer(k)).wait_recv()

    each(nf, af_wait)
    terms = mm(xcat[...], pall[...].reshape(nf * frows, 128)[0 : 64 * TILES, :])
    firsts = terms[0:rpad, :] + terms[rpad : 2 * rpad, :]
    seconds = terms[2 * rpad : 3 * rpad, :] + terms[3 * rpad : 4 * rpad, :]
    update = firsts + pltpu.roll(seconds, 64, 1)
    ou[:, 0, :] = update[0:rows, 0:64]

    each(nf, lambda k: fa_copy(k, fi, f_peer(k)).wait_send())
    each(ns, lambda k: sm_copy(k, si, s_peer(k)).wait_send())
    each(ns, lambda k: sa_copy(k, si, s_peer(k)).wait_send())
    each(nf, lambda k: pr_copy(k, f_peer(k), fi).wait_send())

    def gr_done(k):
        @pl.when(holds(f_peer(k)))
        def _():
            gr_copy(k, f_peer(k), fi).wait_send()

    each(nf, gr_done)

    @pl.when(holds(fi))
    def _():
        each(nf, lambda k: af_copy(k, fi, f_peer(k)).wait_send())

    @pl.when(sec > 0)
    def _():
        send_chain().wait_send()


def make_call(n_sec, nf, ns, grad_type=BF16, early=None):
    rows = ORDER // (nf * ns)
    rpad = pad_to(rows, 16)
    blk = rows * nf
    cw = pad_to(blk, 128)
    frows = 1024 // nf
    srows = frows // ns
    early = n_sec // 2 if early is None else early
    cfg = (n_sec, nf, ns, rows, rpad, early)
    vmem = pltpu.VMEM
    dma = pltpu.SemaphoreType.DMA
    scratch = [
        vmem((ORDER, 128), F32),
        vmem((256, 768), BF16),
        vmem((256, 128), F32),
        vmem((256, 128), F32),
        vmem((768, 128), BF16),
        vmem((256, 128), BF16),
        vmem((256, 128), BF16),
        vmem((768, 128), BF16),
        vmem((rpad, ORDER), BF16),
        vmem((nf, rpad, ORDER), BF16),
        vmem((ORDER, cw), BF16),
        vmem((nf * rpad, cw), BF16),
        vmem((ns, nf * rpad, cw), BF16),
        vmem((ns, 8, 128), F32),
        vmem((ORDER, cw), F32),
        vmem((ORDER, cw), BF16),
        vmem((nf, rpad, ORDER), BF16),
        vmem((nf, rpad, ORDER), BF16),
        vmem((rpad, pad_to(ORDER, 128)), F32),
        vmem((4 * rpad, 64 * TILES), BF16),
        vmem((1024, 128), grad_type),
        vmem((nf, frows, 128), grad_type),
        vmem((ns, srows, 128), F32),
        vmem((ns, srows, 128), F32),
        vmem((srows, 128), BF16),
        vmem((ns, srows, 128), BF16),
        vmem((nf, frows, 128), BF16),
        vmem((128, 128), F32),
        dma, dma,
    ]
    for count in (nf, ns, ns, nf, nf, ns, ns, nf):
        scratch += [dma((count - 1,)), dma((count - 1,))]
    spec = pl.BlockSpec(memory_space=pltpu.VMEM)
    return pl.pallas_call(
        functools.partial(kernel, cfg),
        out_shape=(
            jax.ShapeDtypeStruct((256, 128), BF16),
            jax.ShapeDtypeStruct((rows, 1, 64), F32),
            jax.ShapeDtypeStruct((rows, 1, ORDER), F32),
        ),
        in_specs=[spec] * 6,
        out_specs=(spec, spec, spec),
        scratch_shapes=scratch,
        compiler_params=pltpu.CompilerParams(
            collective_id=0, has_side_effects=True, vmem_limit_bytes=48 * 1024 * 1024
        ),
    )


def build(mesh, nf, ns, early=None):
    n_sec = mesh.shape["section"]

    def shards(acts, preacts, top_grad, weights, a_factor, g_factor):
        call = make_call(n_sec, nf, ns, early=early)
        grads, update, inverse = call(
            acts.reshape(256, 128),
            preacts.reshape(256, 128),
            top_grad.reshape(256, 128),
            weights[0],
            a_factor[0],
            g_factor[0],
        )
        return (
            grads.reshape(acts.shape),
            update.transpose(1, 0, 2),
            inverse.transpose(1, 0, 2),
        )

    placed = (
        P("section", "dp", None, None, None, None, None),
        P("section", "dp", None, None, None, None, None),
        P("dp", None, None, None, None, None),
        P("section", None, None),
        P("section", "dp", None),
        P("section", None, None),
    )
    return jax.shard_map(
        shards,
        mesh=mesh,
        in_specs=placed,
        out_specs=(
            P("section", "dp", None, None, None, None, None),
            P("section", "dp", None),
            P("section", "dp", None),
        ),
        check_vma=False,
    )


def solution(mesh):
    return build(mesh, 8, mesh.shape["dp"] // 8)
```

time: 1170 us -> 128 us (0.11)
  waiting for transfers between devices: 844 us -> 0 us
  blocking collectives: 194 us -> 0 us
  Pallas kernels: 0 us -> 120 us
  local copies, waits for them, and re-layouts: 64.3 us -> 6.97 us
  matrix products: 22.2 us -> 0 us
  other arithmetic: 16.6 us -> 0 us
  between operations: 15.5 us -> 0.65 us
    psum x1 -> x0, waiting for transfers between devices: 613 us -> none  [shards(): summed_grad = lax.psum(local_grad, 'dp')]
    all_gather x1 -> x0, waiting for transfers between devices: 198 us -> none  [shards(): lax.all_gather(resid0, 'dp', axis=0, tiled=True)]
    pmax x1 -> x0, blocking collectives: 194 us -> none  [shards(): step_size = 1.0 / lax.pmax(local_max, 'dp')]
    pallas_call x0 -> x1, Pallas kernels: none -> 120 us  [shards(): call(acts.reshape(256, 128), preacts.reshape(256, 128), top_grad.reshape(...]
    ppermute x8 -> x0, waiting for transfers between devices: 32.9 us -> none  [shifted(): lax.ppermute(value, axis, [(source, source + steps) for source in range(f...]
    while x240 -> x0, local copies, waits for them, and re-layouts: 30.6 us -> none
    dot_general x15 -> x0, matrix products: 22.2 us -> none  [the longest x8 11.9 us: back_input(): lax.dot_general(w_rows, columns, (((0,), (0,)), ((), ())), preferred_elem...]
    broadcast_in_dim x8 -> x0, other arithmetic: 13.5 us -> none  [one_tick(): lax.dynamic_update_index_in_dim(stored_slopes, jnp.where(is_valid, grad_o...]
  transfers between devices with their start and end apart: 10 -> 0, of which waited for: 10 -> 0; matrix products, arithmetic and copies ran while one was open for 0% -> 0% of each run, Pallas kernels for 0% -> 0%
where the time goes in v1:
time: 128 us
  Pallas kernels  120 us (94%)
  local copies, waits for them, and re-layouts  6.97 us (5%)
    pallas_call x1, Pallas kernels, shards(): call(acts.reshape(256, 128), preacts.reshape(256, 128), top_grad.reshape(...  120 us
    unnamed x15, local copies, waits for them, and re-layouts  6.97 us

profile of v1, /device:TPU:6, one launch (start us, length us, event | category | flops | bytes accessed | tf_op | source)
XLA Modules:
  0.0 127.6 jit_solution(15172106289178136538)
XLA Ops:
  0.6 0.0 copy-start
  0.6 0.9 copy-done
  1.6 0.0 copy-start.1
  1.6 0.9 copy-done.1
  2.5 0.0 copy-start.2
  2.5 0.8 copy-done.2
  3.3 0.0 copy-start.3
  3.3 0.8 copy-done.3
  4.2 0.0 copy-start.4
  4.2 0.8 copy-done.4
  5.0 0.0 copy-start.5
  5.0 0.7 copy-done.5
  5.7 120.0 %shard_map.85 = (bf16[256,128]{1,0:T(8,128)(2,1)S(1)}, f32[27,1,64]{2,1,0:T(1,128)S(1)}, f32[27,1,1728]{2,1,0:T(1,128)S(1)}) custom-call(bf16[256,128]{1,0:T(8,128)(2,1)S(1)} %bitcast.12, bf16[256,128]{1,0:T(8,128)(2,1)S(1)} %bitcast.13, bf16[256,128]{1,0:T(8,128)(2,1)S(1)} %bitcast.14, bf16[64,1728]{1,0:T(8,128)(2,1)S(1)} %bitcast.9, ...), custom_call_target="tpu_custom_call" | custom-call | tf_op jit(solution)/shard_map/pallas_call | solution.py:444
  125.7 0.6 copy.12
  126.4 0.6 copy.13
  127.0 0.7 copy.14
Async XLA Ops:
  0.6 0.9 copy-start
  1.6 0.9 copy-start.1
  2.5 0.8 copy-start.2
  3.3 0.8 copy-start.3
  4.2 0.8 copy-start.4
  5.0 0.7 copy-start.5

commit v2 on v1

v2 whole, which is shorter than its diff:
```python
import functools

import jax
import jax.numpy as jnp
from jax import lax
from jax.experimental import pallas as pl
from jax.experimental.pallas import tpu as pltpu
from jax.sharding import PartitionSpec as P

MESH = pl.DeviceIdType.MESH
F32 = jnp.float32
BF16 = jnp.bfloat16
HIGH = lax.Precision.HIGHEST

ORDER = 1728
PAIRED = [((a, 2, c), (a, 0, c)) for a in range(3) for c in range(3)]
MIDDLE = [(a, 1, c) for a in range(3) for c in range(3)]
PAIRED += [(MIDDLE[2 * m], MIDDLE[min(2 * m + 1, 8)]) for m in range(5)]
TILES = len(PAIRED)
PARTS = ("inv", "chain", "red")
EARLY = 2
VMEM_MIB = 56


def tap_of(abc):
    return (abc[0] * 3 + abc[1]) * 3 + abc[2]


def iota(shape, dim):
    return lax.broadcasted_iota(jnp.int32, shape, dim)


def ones_where(mask):
    return jnp.where(mask, 1.0, 0.0).astype(BF16)


def mm(left, right, precision=None):
    return lax.dot_general(
        left, right, (((1,), (0,)), ((), ())), precision=precision, preferred_element_type=F32
    )


def mm_nt(left, right):
    return lax.dot_general(left, right, (((1,), (1,)), ((), ())), preferred_element_type=F32)


def pad_to(value, step):
    return -(-value // step) * step


def kernel(cfg, acts_h, pre_h, top_h, w_h, a_h, gf_h, og, ou, oi, *scratch):
    (
        acts, pre, top, w, a, gf, in_s,
        wt, bw, pre_p, top_p, ash, arr, obuf, gcat, own, apad, sel, squeeze, spc, piece, mx,
        rrow, rcol, pbuf, prc, xf, xcat, wg, rg, sbuf, rs, pall, gbd, stp,
        ch_s, ch_r, fa_s, fa_r, sa_s, sa_r, sm_s, sm_r, pr_s, pr_r,
        gr_s, gr_r, rr_s, rr_r, af_s, af_r,
    ) = scratch
    n_sec, n, rows, rpad, early = cfg
    blk = rows * n
    cw = sel.shape[1]
    frows = rg.shape[1]
    sec = lax.axis_index("section")
    dp = lax.axis_index("dp")
    core = lax.rem(sec, 2)
    low, high = lax.rem(dp, n), dp // n
    fi = low + core * (high - low)
    si = high + core * (low - high)

    def f_dp(index):
        return si * n + index + core * (n - 1) * (index - si)

    def s_dp(index):
        return index * n + fi + core * (n - 1) * (fi - index)

    def f_peer(k):
        return lax.rem(fi + k, n)

    def f_from(k):
        return lax.rem(fi - k + n, n)

    def s_peer(k):
        return lax.rem(si + k, n)

    def s_from(k):
        return lax.rem(si - k + n, n)

    def f_dev(index):
        return (sec, f_dp(index))

    def s_dev(index):
        return (sec, s_dp(index))

    def copy_to(src, dst, ss, rr, k, device):
        return pltpu.make_async_remote_copy(
            src_ref=src, dst_ref=dst, send_sem=ss.at[k - 1], recv_sem=rr.at[k - 1],
            device_id=device, device_id_type=MESH,
        )

    def each(body):
        lax.fori_loop(1, n, lambda k, carry: (body(k), carry)[1], 0)

    def fa_copy(k, slot, index):
        return copy_to(own, apad.at[slot], fa_s, fa_r, k, f_dev(index))

    def sa_copy(k, slot, index, by_column):
        dst = spc.at[:, slot] if by_column else spc.at[slot]
        return copy_to(piece, dst, sa_s, sa_r, k, s_dev(index))

    def sm_copy(k, slot, index):
        return copy_to(mx.at[si], mx.at[slot], sm_s, sm_r, k, s_dev(index))

    def pr_copy(k, chunk, slot):
        return copy_to(pbuf.at[chunk], prc.at[slot], pr_s, pr_r, k, f_dev(chunk))

    def gr_copy(k, chunk, slot):
        return copy_to(wg.at[chunk], rg.at[slot], gr_s, gr_r, k, f_dev(chunk))

    def rr_copy(k, slot, index):
        return copy_to(sbuf, rs.at[slot], rr_s, rr_r, k, s_dev(index))

    def af_copy(k, slot, index):
        return copy_to(pall.at[fi], pall.at[slot], af_s, af_r, k, f_dev(index))

    def send_chain():
        return pltpu.make_async_remote_copy(
            src_ref=obuf, dst_ref=arr, send_sem=ch_s, recv_sem=ch_r,
            device_id=(lax.rem(sec - 1 + n_sec, n_sec), dp), device_id_type=MESH,
        )

    def holds(chunk):
        return chunk * frows < TILES * 64

    inputs = [
        pltpu.make_async_copy(src, dst, in_s.at[m])
        for m, (src, dst) in enumerate(
            [(a_h, a), (w_h, w), (pre_h, pre), (top_h, top), (acts_h, acts), (gf_h, gf)]
        )
    ]

    def conv_matrices():
        wpair = jnp.concatenate([w[...], w[...]], axis=0).astype(F32)
        for m in range(ORDER // 128):
            wt[128 * m : 128 * m + 128, :] = wpair[:, 128 * m : 128 * m + 128].T
        last = 128 * (ORDER // 128)
        wt[last:ORDER, :] = wpair[:, last:ORDER].T
        left64 = iota((64, 128), 1) < 64

        def wtap(aa, b, c):
            start = 64 * tap_of((aa, b, c))
            return wt[start : start + 64, :]

        for c in range(3):
            for x in range(2):
                for y in range(2):
                    for x2 in range(2):
                        block = jnp.where(left64, wtap(x - x2 + 1, y + 1, c), wtap(x - x2 + 1, y, c))
                        row = 64 * (2 * x + y)
                        lane = 256 * c + 128 * x2
                        bw[row : row + 64, lane : lane + 128] = block.astype(BF16)

    def channel_last(forward):
        one, two = (iota((256, 256), 0), iota((256, 256), 1))
        if not forward:
            one, two = two, one
        return ones_where(two == (one & 63) * 4 + (one >> 6))

    def small_inverse():
        dup = ones_where(iota((64, 128), 0) == (iota((64, 128), 1) & 63))
        dup_t = ones_where(iota((128, 64), 1) == (iota((128, 64), 0) & 63))
        wide = mm(mm(dup_t, gf[...]).astype(BF16), dup)
        g_row, g_col = (iota((128, 128), 0), iota((128, 128), 1))
        values = jnp.where((g_row >> 6) == (g_col >> 6), wide, 0.0)
        g_step = 1.0 / jnp.max(jnp.sum(jnp.abs(values), axis=1, keepdims=True), axis=0, keepdims=True)
        g_eye = jnp.where(g_row == g_col, 1.0, 0.0)
        g_res0 = (g_eye - g_step * values).astype(BF16)
        g_res1 = mm(g_res0, g_res0).astype(BF16)
        gbd[...] = g_step * (g_eye + g_res0.astype(F32) + g_res1.astype(F32) + mm(g_res1, g_res0))

    def selections():
        col = iota((ORDER, cw), 1)
        sel[...] = ones_where((iota((ORDER, cw), 0) == fi * blk + col) & (col < blk))
        q_row, q_col = (iota((blk, n * rpad), 0), iota((blk, n * rpad), 1))
        in_slot = lax.rem(q_col, rpad)
        one = ones_where(((q_col // rpad) * rows + in_slot == q_row) & (in_slot < rows)).astype(F32)
        none = jnp.zeros_like(one)
        squeeze[...] = jnp.concatenate(
            [jnp.concatenate([one, none], axis=1), jnp.concatenate([none, one], axis=1)], axis=0
        ).astype(BF16)

    def relay():
        @pl.when(sec < n_sec - 1)
        def _():
            send_chain().wait_recv()
            top_p[...] = arr[...].astype(F32)

        lane = iota((256, 128), 1)
        grad = jnp.where(pre_p[...] > 0, top_p[...], 0.0)
        gcat[256:512, :] = grad.astype(BF16)
        gcat[0:256, :] = jnp.where(lane == 127, 0.0, pltpu.roll(grad, 127, 1)).astype(BF16)
        gcat[512:768, :] = jnp.where(lane == 0, 0.0, pltpu.roll(grad, 1, 1)).astype(BF16)
        obuf[...] = mm(bw[...], gcat[...]).astype(BF16)

        @pl.when(sec > 0)
        def _():
            send_chain().start()

        full = mm_nt(ash[...], gcat[256:512, :])
        left = iota((64, 128), 1) < 64

        def part(aa, c, y):
            total = None
            for x in range(2):
                x2 = x - (aa - 1)
                if 0 <= x2 < 2:
                    row = 256 * c + 64 * (2 * x + y)
                    term = full[row : row + 64, 128 * x2 : 128 * x2 + 128]
                    total = term if total is None else total + term
            return total

        parts = {(aa, c, y): part(aa, c, y) for aa in range(3) for c in range(3) for y in range(2)}
        for m, (one, two) in enumerate(PAIRED):
            if one[1] == 2:
                tile = jnp.where(left, parts[one[0], one[2], 1], parts[one[0], one[2], 0])
            else:
                first = parts[one[0], one[2], 0] + pltpu.roll(parts[one[0], one[2], 1], 64, 1)
                second = pltpu.roll(parts[two[0], two[2], 0], 64, 1) + parts[two[0], two[2], 1]
                tile = jnp.where(left, first, second)
            at = (64 * m) % frows
            wg[(64 * m) // frows, at : at + 64, :] = tile.astype(wg.dtype)

        if "red" in PARTS:
            def start(k):
                @pl.when(holds(f_peer(k)))
                def _():
                    gr_copy(k, f_peer(k), fi).start()

            each(start)
        og[...] = mm(channel_last(False), obuf[...]).astype(BF16)

    def inverse_a():
        def wait(k, largest):
            slot = f_from(k)
            fa_copy(k, slot, f_peer(k)).wait_recv()
            sums = jnp.sum(jnp.abs(apad[slot].astype(F32)), axis=1, keepdims=True)
            return jnp.maximum(largest, sums)

        own_sums = jnp.sum(jnp.abs(own[...].astype(F32)), axis=1, keepdims=True)
        largest = lax.fori_loop(1, n, wait, own_sums)
        mx[si] = jnp.broadcast_to(jnp.max(largest, axis=0, keepdims=True), (8, 128))
        each(lambda k: sm_copy(k, si, s_peer(k)).start())
        piece[...] = mm(apad[...].reshape(n * rpad, ORDER), sel[...]).astype(BF16).reshape(n, rpad, cw)

        @pl.when(core == 0)
        def _():
            each(lambda k: sa_copy(k, si, s_peer(k), False).start())
            spc[si] = piece[...]

        @pl.when(core == 1)
        def _():
            each(lambda k: sa_copy(k, si, s_peer(k), True).start())
            spc[:, si] = piece[...]

        each(lambda k: sm_copy(k, s_from(k), s_peer(k)).wait_recv())
        stp[...] = 1.0 / jnp.broadcast_to(
            jnp.max(jnp.max(mx[...], axis=0), axis=0, keepdims=True), (8, 128)
        )
        step = stp[0:1, 0:1]
        local = iota((rpad, ORDER), 0)
        from_diag = jnp.where(local < rows, iota((rpad, ORDER), 1) - local, -1)

        def residual_rows(u, carry):
            eye = jnp.where(from_diag == f_dp(u) * rows, 1.0, 0.0)
            rrow[u] = (eye - step * apad[u].astype(F32)).astype(BF16)
            return carry

        lax.fori_loop(0, n, residual_rows, 0)

    def inverse_b():
        @pl.when(core == 0)
        def _():
            each(lambda k: sa_copy(k, s_from(k), s_peer(k), False).wait_recv())

        @pl.when(core == 1)
        def _():
            each(lambda k: sa_copy(k, s_from(k), s_peer(k), True).wait_recv())

        step = stp[0:1, 0:1]
        for m in range(n // 2):
            pair = spc[2 * m : 2 * m + 2].reshape(2 * n * rpad, cw)
            at = slice(2 * blk * m, 2 * blk * m + 2 * blk)
            rcol[at, :] = (sel[at, :].astype(F32) - step * mm(squeeze[...], pair)).astype(BF16)
        square = mm(rrow[...].reshape(n * rpad, ORDER), rcol[...]).astype(BF16)
        partial = mm_nt(square, rcol[...]) + mm_nt(square, sel[...])
        pbuf[...] = partial.astype(BF16).reshape(pbuf.shape)
        each(lambda k: pr_copy(k, f_peer(k), fi).start())

    def inverse_c():
        step = stp[0:1, 0:1]
        own_row = iota((rpad, ORDER), 0)
        eye = jnp.where((iota((rpad, ORDER), 1) - own_row == dp * rows) & (own_row < rows), 1.0, 0.0)
        res = (eye - step * own[...].astype(F32)).astype(BF16).astype(F32)
        xf[:, 0:ORDER] = eye + res + pbuf[fi].astype(F32)

        def add(k, carry):
            slot = f_from(k)
            pr_copy(k, f_peer(k), slot).wait_recv()
            xf[:, 0:ORDER] += prc[slot].astype(F32)
            return carry

        lax.fori_loop(1, n, add, 0)
        xf[:, 0:ORDER] = step * xf[:, 0:ORDER]
        oi[:, 0, :] = xf[0:rows, 0:ORDER]
        xf[:, ORDER:] = jnp.zeros((rpad, xf.shape[1] - ORDER), F32)
        left = iota((rpad, 128), 1) < 64

        def tap_lanes(abc, half):
            tap = tap_of(abc)
            group = xf[:, 128 * (tap // 2) : 128 * (tap // 2) + 128]
            return group if tap % 2 == half else pltpu.roll(group, 64, 1)

        for side in range(2):
            for m in range(TILES // 2):
                one, two = (PAIRED[2 * m][side], PAIRED[2 * m + 1][side])
                tile = jnp.where(left, tap_lanes(one, 0), tap_lanes(two, 1))
                if side == 1 and 2 * m + 1 == TILES - 1:
                    tile = jnp.where(left, tile, 0.0)
                first = tile.astype(BF16)
                row = 2 * side * rpad
                xcat[row : row + rpad, 128 * m : 128 * m + 128] = first
                xcat[row + rpad : row + 2 * rpad, 128 * m : 128 * m + 128] = (
                    tile - first.astype(F32)
                ).astype(BF16)

    def reduce_a():
        total = wg[fi].astype(F32)
        each(lambda k: gr_copy(k, fi, f_from(k)).wait_recv())
        for k in range(1, n):
            total = total + rg[f_from(k)].astype(F32)
        sbuf[...] = total.astype(sbuf.dtype)
        each(lambda k: rr_copy(k, si, s_peer(k)).start())

    def reduce_b():
        total = sbuf[...].astype(F32)
        each(lambda k: rr_copy(k, s_from(k), s_peer(k)).wait_recv())
        for k in range(1, n):
            total = total + rs[s_from(k)].astype(F32)
        pall[fi] = mm(total / (n * n), gbd[...], HIGH).astype(BF16)
        each(lambda k: af_copy(k, fi, f_peer(k)).start())

    def finish():
        def wait(k):
            @pl.when(holds(f_from(k)))
            def _():
                af_copy(k, f_from(k), f_peer(k)).wait_recv()

        each(wait)
        terms = mm(xcat[...], pall[...].reshape(n * frows, 128)[0 : 64 * TILES, :])
        firsts = terms[0:rpad, :] + terms[rpad : 2 * rpad, :]
        seconds = terms[2 * rpad : 3 * rpad, :] + terms[3 * rpad : 4 * rpad, :]
        update = firsts + pltpu.roll(seconds, 64, 1)
        ou[:, 0, :] = update[0:rows, 0:64]

    barrier = pltpu.get_barrier_semaphore()
    each(lambda k: pl.semaphore_signal(barrier, inc=1, device_id=f_dev(f_peer(k)), device_id_type=MESH))
    each(lambda k: pl.semaphore_signal(barrier, inc=1, device_id=s_dev(s_peer(k)), device_id_type=MESH))
    for near in (sec + 1, sec + n_sec - 1):
        pl.semaphore_signal(
            barrier, inc=1, device_id=(lax.rem(near, n_sec), dp), device_id_type=MESH
        )

    for one in inputs:
        one.start()
    inputs[0].wait()
    own[...] = jnp.zeros_like(own)
    own[0:rows, :] = a[...]
    inputs[1].wait()
    conv_matrices()
    for one in inputs[2:]:
        one.wait()
    pre_p[...] = mm(channel_last(True), pre[...])
    top_p[...] = mm(channel_last(True), top[...])
    pl.semaphore_wait(barrier, 2 * n)

    if "inv" in PARTS:
        each(lambda k: fa_copy(k, fi, f_peer(k)).start())
        apad[fi] = own[...]

    lanes = iota((256, 128), 1)
    act_p = mm(channel_last(True), acts[...])
    ash[0:256, :] = jnp.where(lanes == 0, 0.0, pltpu.roll(act_p, 1, 1)).astype(BF16)
    ash[256:512, :] = act_p.astype(BF16)
    ash[512:768, :] = jnp.where(lanes == 127, 0.0, pltpu.roll(act_p, 127, 1)).astype(BF16)
    if wg.shape[0] * frows > 64 * TILES:
        wg[n - 1, frows - (1024 - 64 * TILES) :, :] = jnp.zeros((1024 - 64 * TILES, 128), wg.dtype)

    if "chain" in PARTS:
        pl.when(sec >= early)(relay)
    selections()
    small_inverse()
    if "inv" in PARTS:
        inverse_a()
    if "chain" in PARTS:
        pl.when(sec < early)(relay)
    if "red" in PARTS:
        pl.when(holds(fi))(reduce_a)
    if "inv" in PARTS:
        inverse_b()
    if "red" in PARTS:
        pl.when(holds(fi))(reduce_b)
    if "inv" in PARTS:
        inverse_c()
    if "red" in PARTS:
        finish()

    if "inv" in PARTS:
        each(lambda k: fa_copy(k, fi, f_peer(k)).wait_send())
        each(lambda k: sm_copy(k, si, s_peer(k)).wait_send())

        @pl.when(core == 0)
        def _():
            each(lambda k: sa_copy(k, si, s_peer(k), False).wait_send())

        @pl.when(core == 1)
        def _():
            each(lambda k: sa_copy(k, si, s_peer(k), True).wait_send())

        each(lambda k: pr_copy(k, f_peer(k), fi).wait_send())

    if "red" in PARTS:
        def gr_done(k):
            @pl.when(holds(f_peer(k)))
            def _():
                gr_copy(k, f_peer(k), fi).wait_send()

        each(gr_done)

        @pl.when(holds(fi))
        def _():
            each(lambda k: rr_copy(k, si, s_peer(k)).wait_send())
            each(lambda k: af_copy(k, fi, f_peer(k)).wait_send())

    if "chain" in PARTS:
        @pl.when(sec > 0)
        def _():
            send_chain().wait_send()


def make_call(n_sec, n, early, grad_type=BF16):
    rows = ORDER // (n * n)
    rpad = pad_to(rows, 16)
    blk = rows * n
    cw = pad_to(blk, 128)
    frows = 1024 // n
    cfg = (n_sec, n, rows, rpad, early)
    vmem = pltpu.VMEM
    dma = pltpu.SemaphoreType.DMA
    scratch = [
        vmem((256, 128), BF16),
        vmem((256, 128), BF16),
        vmem((256, 128), BF16),
        vmem((64, ORDER), BF16),
        vmem((rows, ORDER), BF16),
        vmem((64, 64), BF16),
        dma((6,)),
        vmem((ORDER, 128), F32),
        vmem((256, 768), BF16),
        vmem((256, 128), F32),
        vmem((256, 128), F32),
        vmem((768, 128), BF16),
        vmem((256, 128), BF16),
        vmem((256, 128), BF16),
        vmem((768, 128), BF16),
        vmem((rpad, ORDER), BF16),
        vmem((n, rpad, ORDER), BF16),
        vmem((ORDER, cw), BF16),
        vmem((2 * blk, 2 * n * rpad), BF16),
        vmem((n, n, rpad, cw), BF16),
        vmem((n, rpad, cw), BF16),
        vmem((n, 8, 128), F32),
        vmem((n, rpad, ORDER), BF16),
        vmem((ORDER, cw), BF16),
        vmem((n, rpad, ORDER), BF16),
        vmem((n, rpad, ORDER), BF16),
        vmem((rpad, pad_to(ORDER, 128)), F32),
        vmem((4 * rpad, 64 * TILES), BF16),
        vmem((n, frows, 128), grad_type),
        vmem((n, frows, 128), grad_type),
        vmem((frows, 128), grad_type),
        vmem((n, frows, 128), grad_type),
        vmem((n, frows, 128), BF16),
        vmem((128, 128), F32),
        vmem((8, 128), F32),
        dma, dma,
    ]
    scratch += [dma((n - 1,)) for _ in range(14)]
    hbm = pl.BlockSpec(memory_space=pltpu.HBM)
    spec = pl.BlockSpec(memory_space=pltpu.VMEM)
    return pl.pallas_call(
        functools.partial(kernel, cfg),
        out_shape=(
            jax.ShapeDtypeStruct((256, 128), BF16),
            jax.ShapeDtypeStruct((rows, 1, 64), F32),
            jax.ShapeDtypeStruct((rows, 1, ORDER), F32),
        ),
        in_specs=[hbm] * 6,
        out_specs=(spec, spec, spec),
        scratch_shapes=scratch,
        compiler_params=pltpu.CompilerParams(
            collective_id=0, has_side_effects=True, vmem_limit_bytes=VMEM_MIB * 1024 * 1024
        ),
    )


def build(mesh, n, early):
    n_sec = mesh.shape["section"]

    def shards(acts, preacts, top_grad, weights, a_factor, g_factor):
        call = make_call(n_sec, n, early)
        grads, update, inverse = call(
            acts.reshape(256, 128),
            preacts.reshape(256, 128),
            top_grad.reshape(256, 128),
            weights[0],
            a_factor[0],
            g_factor[0],
        )
        return (
            grads.reshape(acts.shape),
            update.transpose(1, 0, 2),
            inverse.transpose(1, 0, 2),
        )

    placed = (
        P("section", "dp", None, None, None, None, None),
        P("section", "dp", None, None, None, None, None),
        P("dp", None, None, None, None, None),
        P("section", None, None),
        P("section", "dp", None),
        P("section", None, None),
    )
    return jax.shard_map(
        shards,
        mesh=mesh,
        in_specs=placed,
        out_specs=(
            P("section", "dp", None, None, None, None, None),
            P("section", "dp", None),
            P("section", "dp", None),
        ),
        check_vma=False,
    )


def solution(mesh):
    return build(mesh, 8, EARLY)
```

time: 128 us -> 78.9 us (0.62)
  Pallas kernels: 120 us -> 73.1 us
  local copies, waits for them, and re-layouts: 6.97 us -> 3.75 us
    pallas_call x1, Pallas kernels: 120 us -> 73.1 us  [shards(): call(acts.reshape(256, 128), preacts.reshape(256, 128), top_grad.reshape(...]
    unnamed x15 -> x5, local copies, waits for them, and re-layouts: 6.97 us -> 3.75 us
where the time goes in v2:
time: 78.9 us; the launch traced here: 77.5 us
  Pallas kernels  73.1 us (93%)
  local copies, waits for them, and re-layouts  3.75 us (5%)
    pallas_call x1, Pallas kernels, shards(): call(acts.reshape(256, 128), preacts.reshape(256, 128), top_grad.reshape(...  73.1 us
    unnamed x5, local copies, waits for them, and re-layouts  3.75 us

profile of v2, /device:TPU:6, one launch (start us, length us, event | category | flops | bytes accessed | tf_op | source)
XLA Modules:
  0.0 77.5 jit_solution(3186293224324088786)
XLA Ops:
  0.6 73.1 %shard_map.85 = (bf16[256,128]{1,0:T(8,128)(2,1)}, f32[27,1,64]{2,1,0:T(1,128)}, f32[27,1,1728]{2,1,0:T(1,128)}) custom-call(bf16[256,128]{1,0:T(8,128)(2,1)} %bitcast.12, bf16[256,128]{1,0:T(8,128)(2,1)} %bitcast.13, bf16[256,128]{1,0:T(8,128)(2,1)} %bitcast.14, bf16[64,1728]{1,0:T(8,128)(2,1)} %bitcast.9, bf16[27,1728]{1,0:T(8,128)(2,1)} %bitcast.11, ...), custom_call_target="tpu_custom_call" | custom-call | tf_op jit(solution)/shard_map/pallas_call | solution.py:520
  73.7 0.0 copy-start
  73.7 1.5 %copy.12 = bf16[1,1,1,64,2,2,128]{6,5,4,3,2,1,0:T(2,128)(2,1)} copy(bf16[1,1,1,64,2,2,128]{6,5,4,3,2,1,0:T(2,128)(2,1)} %bitcast.15) | data formatting | bytes 131072
  75.2 0.0 copy-done
  75.2 0.6 copy.13
  75.8 1.6 %copy.14 = f32[1,27,1728]{2,0,1:T(1,128)} copy(f32[1,27,1728]{2,0,1:T(1,128)} %bitcast.10) | data formatting | bytes 373248
Async XLA Ops:
  73.7 1.5 %copy-start = (f32[27,1,64]{2,1,0:T(1,128)S(1)}, f32[27,1,64]{2,1,0:T(1,128)}, u32[]{:S(2)}) copy-start(f32[27,1,64]{2,1,0:T(1,128)} %get-tuple-element.7) | copy-start | bytes 20740

commit v3 on v2

--- a/solution.py
+++ b/solution.py
@@ -18,7 +18,8 @@
 PAIRED += [(MIDDLE[2 * m], MIDDLE[min(2 * m + 1, 8)]) for m in range(5)]
 TILES = len(PAIRED)
 PARTS = ("inv", "chain", "red")
-EARLY = 2
+PASS = 4
+LATE_CONV = 0
 VMEM_MIB = 56
 
 
@@ -51,14 +52,14 @@
 def kernel(cfg, acts_h, pre_h, top_h, w_h, a_h, gf_h, og, ou, oi, *scratch):
     (
         acts, pre, top, w, a, gf, in_s,
-        wt, bw, pre_p, top_p, ash, arr, obuf, gcat, own, apad, sel, squeeze, spc, piece, mx,
-        rrow, rcol, pbuf, prc, xf, xcat, wg, rg, sbuf, rs, pall, gbd, stp,
+        wt, bw, pre_p, top_p, ash, arr, obuf, gcat, own, apad, squeeze, spc, piece, mx,
+        rrow, both, pbuf, prc, xf, xcat, wg, rg, sbuf, rs, pall, gbd, stp,
         ch_s, ch_r, fa_s, fa_r, sa_s, sa_r, sm_s, sm_r, pr_s, pr_r,
         gr_s, gr_r, rr_s, rr_r, af_s, af_r,
     ) = scratch
-    n_sec, n, rows, rpad, early = cfg
+    n_sec, n, rows, rpad = cfg
     blk = rows * n
-    cw = sel.shape[1]
+    cw = both.shape[1] // 2
     frows = rg.shape[1]
     sec = lax.axis_index("section")
     dp = lax.axis_index("dp")
@@ -73,17 +74,35 @@
     def s_dp(index):
         return index * n + fi + core * (n - 1) * (fi - index)
 
+    ns = n // 2
+
+    def along(index, k, way):
+        far = ns + (k // 2) * (2 * lax.rem(k, 2) - 1)
+        return lax.rem(index + way * far + n, n)
+
+    def across(index, k, way):
+        same = k // (ns + 1)
+        plane, x = index // ns, lax.rem(index, ns)
+        step = k - 1 - (ns - 1) * same
+        return (plane + (1 - same) * (1 - 2 * plane)) * ns + lax.rem(x + way * step + ns, ns)
+
+    def f_near(k, way):
+        return along(fi, k, way) + core * (across(fi, k, way) - along(fi, k, way))
+
+    def s_near(k, way):
+        return across(si, k, way) + core * (along(si, k, way) - across(si, k, way))
+
     def f_peer(k):
-        return lax.rem(fi + k, n)
+        return f_near(k, 1)
 
     def f_from(k):
-        return lax.rem(fi - k + n, n)
+        return f_near(k, -1)
 
     def s_peer(k):
-        return lax.rem(si + k, n)
+        return s_near(k, 1)
 
     def s_from(k):
-        return lax.rem(si - k + n, n)
+        return s_near(k, -1)
 
     def f_dev(index):
         return (sec, f_dp(index))
@@ -102,6 +121,19 @@
 
     def fa_copy(k, slot, index):
         return copy_to(own, apad.at[slot], fa_s, fa_r, k, f_dev(index))
+
+    def fx_copy(k):
+        partner = f_from(1)
+        plane, x = fi // ns, lax.rem(fi, ns)
+        return copy_to(
+            apad.at[partner], apad.at[partner], fa_s, fa_r, k,
+            f_dev(plane * ns + lax.rem(x + k - 1, ns)),
+        )
+
+    def pass_on():
+        fa_copy(1, f_from(1), f_peer(1)).wait_recv()
+        for k in range(2, ns + 1):
+            fx_copy(k).start()
 
     def sa_copy(k, slot, index, by_column):
         dst = spc.at[:, slot] if by_column else spc.at[slot]
@@ -179,7 +211,7 @@
 
     def selections():
         col = iota((ORDER, cw), 1)
-        sel[...] = ones_where((iota((ORDER, cw), 0) == fi * blk + col) & (col < blk))
+        both[:, cw:] = ones_where((iota((ORDER, cw), 0) == fi * blk + col) & (col < blk))
         q_row, q_col = (iota((blk, n * rpad), 0), iota((blk, n * rpad), 1))
         in_slot = lax.rem(q_col, rpad)
         one = ones_where(((q_col // rpad) * rows + in_slot == q_row) & (in_slot < rows)).astype(F32)
@@ -241,7 +273,11 @@
     def inverse_a():
         def wait(k, largest):
             slot = f_from(k)
-            fa_copy(k, slot, f_peer(k)).wait_recv()
+
+            @pl.when((core == 0) | (k > 1))
+            def _():
+                fa_copy(k, slot, f_peer(k)).wait_recv()
+
             sums = jnp.sum(jnp.abs(apad[slot].astype(F32)), axis=1, keepdims=True)
             return jnp.maximum(largest, sums)
 
@@ -249,7 +285,7 @@
         largest = lax.fori_loop(1, n, wait, own_sums)
         mx[si] = jnp.broadcast_to(jnp.max(largest, axis=0, keepdims=True), (8, 128))
         each(lambda k: sm_copy(k, si, s_peer(k)).start())
-        piece[...] = mm(apad[...].reshape(n * rpad, ORDER), sel[...]).astype(BF16).reshape(n, rpad, cw)
+        piece[...] = mm(apad[...].reshape(n * rpad, ORDER), both[:, cw:]).astype(BF16).reshape(n, rpad, cw)
 
         @pl.when(core == 0)
         def _():
@@ -289,9 +325,9 @@
         for m in range(n // 2):
             pair = spc[2 * m : 2 * m + 2].reshape(2 * n * rpad, cw)
             at = slice(2 * blk * m, 2 * blk * m + 2 * blk)
-            rcol[at, :] = (sel[at, :].astype(F32) - step * mm(squeeze[...], pair)).astype(BF16)
-        square = mm(rrow[...].reshape(n * rpad, ORDER), rcol[...]).astype(BF16)
-        partial = mm_nt(square, rcol[...]) + mm_nt(square, sel[...])
+            both[at, 0:cw] = (both[at, cw:].astype(F32) - step * mm(squeeze[...], pair)).astype(BF16)
+        square = mm(rrow[...].reshape(n * rpad, ORDER), both[:, 0:cw]).astype(BF16)
+        partial = mm_nt(jnp.concatenate([square, square], axis=1), both[...])
         pbuf[...] = partial.astype(BF16).reshape(pbuf.shape)
         each(lambda k: pr_copy(k, f_peer(k), fi).start())
 
@@ -374,17 +410,32 @@
     inputs[0].wait()
     own[...] = jnp.zeros_like(own)
     own[0:rows, :] = a[...]
-    inputs[1].wait()
-    conv_matrices()
-    for one in inputs[2:]:
-        one.wait()
-    pre_p[...] = mm(channel_last(True), pre[...])
-    top_p[...] = mm(channel_last(True), top[...])
+    def prologue():
+        inputs[1].wait()
+        conv_matrices()
+        for one in inputs[2:]:
+            one.wait()
+        pre_p[...] = mm(channel_last(True), pre[...])
+        top_p[...] = mm(channel_last(True), top[...])
+
+    if not LATE_CONV:
+        prologue()
     pl.semaphore_wait(barrier, 2 * n)
 
     if "inv" in PARTS:
-        each(lambda k: fa_copy(k, fi, f_peer(k)).start())
+        @pl.when(core == 0)
+        def _():
+            each(lambda k: fa_copy(k, fi, f_peer(k)).start())
+
+        @pl.when(core == 1)
+        def _():
+            for k in range(1, n):
+                if k == 1 or k > ns:
+                    fa_copy(k, fi, f_peer(k)).start()
+
         apad[fi] = own[...]
+    if LATE_CONV:
+        prologue()
 
     lanes = iota((256, 128), 1)
     act_p = mm(channel_last(True), acts[...])
@@ -394,14 +445,16 @@
     if wg.shape[0] * frows > 64 * TILES:
         wg[n - 1, frows - (1024 - 64 * TILES) :, :] = jnp.zeros((1024 - 64 * TILES, 128), wg.dtype)
 
+    if "inv" in PARTS:
+        pl.when((core == 1) & (sec < PASS))(pass_on)
     if "chain" in PARTS:
-        pl.when(sec >= early)(relay)
+        relay()
+    if "inv" in PARTS:
+        pl.when((core == 1) & (sec >= PASS))(pass_on)
     selections()
     small_inverse()
     if "inv" in PARTS:
         inverse_a()
-    if "chain" in PARTS:
-        pl.when(sec < early)(relay)
     if "red" in PARTS:
         pl.when(holds(fi))(reduce_a)
     if "inv" in PARTS:
@@ -414,7 +467,15 @@
         finish()
 
     if "inv" in PARTS:
-        each(lambda k: fa_copy(k, fi, f_peer(k)).wait_send())
+        @pl.when(core == 0)
+        def _():
+            each(lambda k: fa_copy(k, fi, f_peer(k)).wait_send())
+
+        @pl.when(core == 1)
+        def _():
+            for k in range(1, n):
+                (fx_copy(k) if 1 < k <= ns else fa_copy(k, fi, f_peer(k))).wait_send()
+
         each(lambda k: sm_copy(k, si, s_peer(k)).wait_send())
 
         @pl.when(core == 0)
@@ -446,13 +507,13 @@
             send_chain().wait_send()
 
 
-def make_call(n_sec, n, early, grad_type=BF16):
+def make_call(n_sec, n, grad_type=BF16):
     rows = ORDER // (n * n)
     rpad = pad_to(rows, 16)
     blk = rows * n
     cw = pad_to(blk, 128)
     frows = 1024 // n
-    cfg = (n_sec, n, rows, rpad, early)
+    cfg = (n_sec, n, rows, rpad)
     vmem = pltpu.VMEM
     dma = pltpu.SemaphoreType.DMA
     scratch = [
@@ -473,13 +534,12 @@
         vmem((768, 128), BF16),
         vmem((rpad, ORDER), BF16),
         vmem((n, rpad, ORDER), BF16),
-        vmem((ORDER, cw), BF16),
         vmem((2 * blk, 2 * n * rpad), BF16),
         vmem((n, n, rpad, cw), BF16),
         vmem((n, rpad, cw), BF16),
         vmem((n, 8, 128), F32),
         vmem((n, rpad, ORDER), BF16),
-        vmem((ORDER, cw), BF16),
+        vmem((ORDER, 2 * cw), BF16),
         vmem((n, rpad, ORDER), BF16),
         vmem((n, rpad, ORDER), BF16),
         vmem((rpad, pad_to(ORDER, 128)), F32),
@@ -512,11 +572,11 @@
     )
 
 
-def build(mesh, n, early):
+def build(mesh, n):
     n_sec = mesh.shape["section"]
 
     def shards(acts, preacts, top_grad, weights, a_factor, g_factor):
-        call = make_call(n_sec, n, early)
+        call = make_call(n_sec, n)
         grads, update, inverse = call(
             acts.reshape(256, 128),
             preacts.reshape(256, 128),
@@ -553,4 +613,4 @@
 
 
 def solution(mesh):
-    return build(mesh, 8, EARLY)
+    return build(mesh, 8)

time: 78.9 us -> 74.9 us (0.949)
  Pallas kernels: 73.1 us -> 69.7 us
    pallas_call x1, Pallas kernels: 73.1 us -> 69.7 us  [shards(): call(acts.reshape(256, 128), preacts.reshape(256, 128), top_grad.reshape(...]
where the time goes in v3:
time: 74.9 us; the launch traced here: 74.1 us
  Pallas kernels  69.7 us (93%)
  local copies, waits for them, and re-layouts  3.75 us (5%)
    pallas_call x1, Pallas kernels, shards(): call(acts.reshape(256, 128), preacts.reshape(256, 128), top_grad.reshape(...  69.7 us
    unnamed x5, local copies, waits for them, and re-layouts  3.75 us

profile of v3, /device:TPU:6, one launch (start us, length us, event | category | flops | bytes accessed | tf_op | source)
XLA Modules:
  0.0 74.1 jit_solution(801611029849040945)
XLA Ops:
  0.6 69.7 %shard_map.85 = (bf16[256,128]{1,0:T(8,128)(2,1)}, f32[27,1,64]{2,1,0:T(1,128)}, f32[27,1,1728]{2,1,0:T(1,128)}) custom-call(bf16[256,128]{1,0:T(8,128)(2,1)} %bitcast.12, bf16[256,128]{1,0:T(8,128)(2,1)} %bitcast.13, bf16[256,128]{1,0:T(8,128)(2,1)} %bitcast.14, bf16[64,1728]{1,0:T(8,128)(2,1)} %bitcast.9, bf16[27,1728]{1,0:T(8,128)(2,1)} %bitcast.11, ...), custom_call_target="tpu_custom_call" | custom-call | tf_op jit(solution)/shard_map/pallas_call | solution.py:580
  70.4 0.0 copy-start
  70.4 1.5 %copy.12 = bf16[1,1,1,64,2,2,128]{6,5,4,3,2,1,0:T(2,128)(2,1)} copy(bf16[1,1,1,64,2,2,128]{6,5,4,3,2,1,0:T(2,128)(2,1)} %bitcast.15) | data formatting | bytes 131072
  71.9 0.0 copy-done
  71.9 0.6 copy.13
  72.5 1.6 %copy.14 = f32[1,27,1728]{2,0,1:T(1,128)} copy(f32[1,27,1728]{2,0,1:T(1,128)} %bitcast.10) | data formatting | bytes 373248
Async XLA Ops:
  70.4 1.5 %copy-start = (f32[27,1,64]{2,1,0:T(1,128)S(1)}, f32[27,1,64]{2,1,0:T(1,128)}, u32[]{:S(2)}) copy-start(f32[27,1,64]{2,1,0:T(1,128)} %get-tuple-element.7) | copy-start | bytes 20740
